TPU v7x, 32 devices: a whole 2x2x4 slice. The times are simulated.
32 devices in a mesh: pb: 4 (over z), pa: 8 (over y, x, core).
Axes of the slice: x: 2, y: 2, z: 4, core: 2. Of those that a mesh axis runs over, the one named last changes fastest.
Arguments:
- query_states: bfloat16 [128, 32, 768], P(('pb', 'pa')), may hold values from -6 to 6
- passage_states: bfloat16 [1024, 180, 768], P(('pb', 'pa')), may hold values from -6 to 6
- head: bfloat16 [768, 128], replicated, may hold values from -0.21875 to 0.21875
- teacher: float32 [128, 32], P(('pb', 'pa')), may hold values from -8 to 8
- cand_owner: int32 [128, 32], P(('pb', 'pa')), may hold values from 0 to 31, all different within a row; in each aligned block of 4 rows (0 to 3, 4 to 7, ...) at most 4 rows name the same one
- cand_local: int32 [128, 32], P(('pb', 'pa')), may hold values from 0 to 31
- query_lengths: int32 [128], P(('pb', 'pa')), may hold values from 1 to 32, 3072 in all
- passage_lengths: int32 [1024], P(('pb', 'pa')), may hold values from 1 to 180, 122880 in all
Outputs:
- scores: float32 [128, 32], P(('pb', 'pa'))
- loss: float32 [], replicated
- head_grad: float32 [768, 128], replicated
Inputs may be any that keep to these rules, and one draw needn't show every extreme that they name: `cand_owner`: each row names 32 different devices; among the rows of one device no device is named by more than 4 rows.
All inputs are finite; a program needn't handle non-finite values. No bound on the sum of `query_lengths` or of `passage_lengths` on one device may be relied on, other than what follows from the above.
Results may differ from a plain program's by a relative error of at most 0.0078.
Values may be sent and summed in bfloat16 or wider, within the bound.
A program may use at most 192 MiB of HBM per device.

v0:
```python
import functools

import jax
import jax.numpy as jnp
from jax import lax
from jax.experimental import pallas as pl
from jax.experimental.pallas import tpu as pltpu
from jax.sharding import PartitionSpec as P

MESH = pl.DeviceIdType.MESH
F32 = jnp.float32
BF16 = jnp.bfloat16
LANES = 128

SOFTMAX_TEMP = 0.05
EPSILON = 1e-06


def embed(states, head):
    flat_states = states.reshape(-1, states.shape[-1])
    projected = jnp.dot(flat_states, head, preferred_element_type=jnp.float32)
    norm_value = jnp.sqrt(jnp.sum(projected * projected, axis=-1, keepdims=True) + EPSILON)
    unit_rows = projected / norm_value
    embedded = unit_rows.astype(jnp.bfloat16).reshape(states.shape[0], states.shape[1], -1)
    return (embedded, unit_rows, norm_value)


def head_term(states, unit_rows, norm_value, grads):
    flat_states = states.reshape(unit_rows.shape[0], -1)
    along = grads.reshape(unit_rows.shape)
    radial = jnp.sum(along * unit_rows, axis=-1, keepdims=True)
    grad_pre = ((along - unit_rows * radial) / norm_value).astype(jnp.bfloat16)
    return lax.dot_general(
        flat_states, grad_pre, (((0,), (0,)), ((), ())), preferred_element_type=jnp.float32
    )


def length_mask(lengths, width_value):
    return (jnp.arange(width_value, dtype=jnp.int32)[None, :] < lengths[:, None]).astype(
        jnp.float32
    )


def pair_terms(query_rows, passage_rows, passage_token_mask):
    token_similarity = jnp.einsum(
        "sid,sjd->sij", query_rows, passage_rows, preferred_element_type=jnp.float32
    )
    exponent_terms = jnp.exp(token_similarity / SOFTMAX_TEMP) * passage_token_mask[:, None, :]
    return (exponent_terms, jnp.sum(exponent_terms, axis=-1))


def pair_scores(exponent_total, query_token_mask):
    return jnp.sum(query_token_mask * (SOFTMAX_TEMP * jnp.log(exponent_total)), axis=-1)


def pair_grads(exponent_terms, exponent_total, query_token_mask, weights, query_rows, passage_rows):
    share = (
        (weights[:, None] * query_token_mask / exponent_total)[:, :, None] * exponent_terms
    ).astype(jnp.bfloat16)
    query_part = jnp.einsum(
        "sij,sjd->sid", share, passage_rows, preferred_element_type=jnp.float32
    ).astype(jnp.bfloat16)
    passage_part = jnp.einsum(
        "sij,sid->sjd", share, query_rows, preferred_element_type=jnp.float32
    ).astype(jnp.bfloat16)
    return (query_part, passage_part)


def distill(scores, teacher):
    student_exp = jnp.exp(scores)
    student_sum = jnp.sum(student_exp, axis=-1, keepdims=True)
    teacher_exp = jnp.exp(teacher)
    teacher_sum = jnp.sum(teacher_exp, axis=-1, keepdims=True)
    target = teacher_exp / teacher_sum
    divergence = jnp.sum(
        target * (teacher - jnp.log(teacher_sum) - (scores - jnp.log(student_sum))), axis=-1
    )
    return (student_exp / student_sum - target, divergence)


def accumulate(parts, local_index, passages):
    onehot_rows = (local_index[:, None] == jnp.arange(passages, dtype=jnp.int32)[None, :]).astype(
        jnp.bfloat16
    )
    summed = jnp.einsum(
        "sp,sx->px",
        onehot_rows,
        parts.reshape(parts.shape[0], -1),
        preferred_element_type=jnp.float32,
    )
    return summed.reshape((passages,) + parts.shape[1:])


def slot_plan(owners, capacity, devices):
    hits = (owners[:, :, None] == jnp.arange(devices, dtype=jnp.int32)[None, None, :]).astype(
        jnp.int32
    )
    present = jnp.sum(hits, axis=1)
    earlier = jnp.cumsum(present, axis=0) - present
    rank_value = jnp.sum(hits * earlier[:, None, :], axis=2)
    return owners * capacity + rank_value


def on_device(
    query_states,
    passage_states,
    head,
    teacher,
    cand_owner,
    cand_local,
    query_lengths,
    passage_lengths,
):
    outer_size = lax.axis_size("pb")
    inner_size = lax.axis_size("pa")
    devices = outer_size * inner_size
    queries = query_states.shape[0]
    query_len = query_states.shape[1]
    passages = passage_states.shape[0]
    passage_len = passage_states.shape[1]
    candidates = cand_owner.shape[1]
    capacity = min(queries, max(2, 2 * queries * candidates // devices))
    slots = devices * capacity
    query_emb, query_unit, query_norm = embed(query_states, head)
    slot_index = slot_plan(cand_owner, capacity, devices)
    flat_slot = slot_index.reshape(-1)
    row_of = jnp.repeat(jnp.arange(queries, dtype=jnp.int32), candidates)
    slot_live = jnp.zeros((slots,), jnp.int32).at[flat_slot].set(1)
    slot_query = jnp.zeros((slots,), jnp.int32).at[flat_slot].set(row_of)
    slot_local = jnp.zeros((slots,), jnp.int32).at[flat_slot].set(cand_local.reshape(-1))
    passage_emb, passage_unit, passage_norm = embed(passage_states, head)
    sent_emb = query_emb.reshape(queries, -1)[slot_query]
    sent_len = query_lengths[slot_query] * slot_live
    got_emb, got_local, got_len = (
        lax.all_to_all(
            sent_emb.reshape(devices, capacity, -1),
            ("pb", "pa"),
            split_axis=0,
            concat_axis=0,
            tiled=True,
        ),
        lax.all_to_all(
            slot_local.reshape(devices, capacity),
            ("pb", "pa"),
            split_axis=0,
            concat_axis=0,
            tiled=True,
        ),
        lax.all_to_all(
            sent_len.reshape(devices, capacity),
            ("pb", "pa"),
            split_axis=0,
            concat_axis=0,
            tiled=True,
        ),
    )
    recv_emb = got_emb.reshape(slots, query_len, -1)
    recv_local = got_local.reshape(slots)
    recv_mask = length_mask(got_len.reshape(slots), query_len)
    passage_rows = passage_emb[recv_local]
    passage_token_mask = length_mask(passage_lengths[recv_local], passage_len)
    exponent_terms, exponent_total = pair_terms(recv_emb, passage_rows, passage_token_mask)
    slot_scores = pair_scores(exponent_total, recv_mask)
    returned_scores = lax.all_to_all(
        slot_scores.reshape(devices, capacity),
        ("pb", "pa"),
        split_axis=0,
        concat_axis=0,
        tiled=True,
    )
    scores = returned_scores.reshape(slots)[slot_index]
    weights, divergence = distill(scores, teacher)
    sent_weight = jnp.zeros((slots,), jnp.float32).at[flat_slot].set(weights.reshape(-1))
    recv_weight = lax.all_to_all(
        sent_weight.reshape(devices, capacity),
        ("pb", "pa"),
        split_axis=0,
        concat_axis=0,
        tiled=True,
    ).reshape(slots)
    query_part, passage_part = pair_grads(
        exponent_terms, exponent_total, recv_mask, recv_weight, recv_emb, passage_rows
    )
    passage_grad = accumulate(passage_part, recv_local, passages)
    returned_grads = lax.all_to_all(
        query_part.reshape(devices, capacity, -1),
        ("pb", "pa"),
        split_axis=0,
        concat_axis=0,
        tiled=True,
    )
    query_terms = returned_grads.reshape(slots, query_len, -1)[slot_index]
    query_grad = jnp.sum(query_terms.astype(jnp.float32), axis=1)
    local_grad = head_term(query_states, query_unit, query_norm, query_grad) + head_term(
        passage_states, passage_unit, passage_norm, passage_grad
    )
    head_grad, divergence_total = lax.psum((local_grad, jnp.sum(divergence)), ("pb", "pa"))
    loss = divergence_total / (queries * devices)
    return (scores, loss, head_grad)


def radices(size):
    found = []
    if (size.bit_length() - 1) % 2:
        found.append(2)
        size //= 2
    while size > 1:
        found.append(4)
        size //= 4
    return found


def exchange_stages(outer, inner):
    stages = []
    held = 1
    stride = 1
    for radix in radices(outer):
        stages.append(("pb", stride, radix, held))
        stride *= radix
        held *= radix
    inner_radices = radices(inner)
    strides = []
    stride = 1
    for radix in inner_radices:
        strides.append(stride)
        stride *= radix
    for radix, stride in zip(inner_radices[::-1], strides[::-1]):
        stages.append(("pa", stride, radix, held))
        held *= radix
    return stages


def rank_of(stages, coordinates):
    rank = 0
    for axis, stride, radix, held in stages:
        rank = rank + (coordinates[axis] // stride) % radix * held
    return rank


def here():
    return {"pb": lax.axis_index("pb"), "pa": lax.axis_index("pa")}


class Stage:
    def __init__(self, stage, at):
        self.axis, self.stride, self.radix, self.held = stage
        self.at = at
        self.digit = (at[self.axis] // self.stride) % self.radix

    def peers(self):
        found = []
        for step in range(1, self.radix):
            other = (self.digit + step) % self.radix
            place = dict(self.at)
            place[self.axis] = self.at[self.axis] + (other - self.digit) * self.stride
            found.append((step - 1, other, (place["pb"], place["pa"])))
        return found


def greet(stages):
    barrier = pltpu.get_barrier_semaphore()
    count = 0
    for stage in stages:
        for _, _, device in stage.peers():
            pl.semaphore_signal(barrier, inc=1, device_id=device, device_id_type=MESH)
            count += 1
    return barrier, count


def send(source, target, send_sem, recv_sem, device):
    copy = pltpu.make_async_remote_copy(
        src_ref=source,
        dst_ref=target,
        send_sem=send_sem,
        recv_sem=recv_sem,
        device_id=device,
        device_id_type=MESH,
    )
    copy.start()
    return copy


def gather_step(stage, rank, ref, unit, send_sems, recv_sems, base):
    first = rank // stage.held * stage.held * unit
    block = ref.at[pl.ds(first, stage.held * unit)]
    return [
        send(block, block, send_sems.at[base + slot], recv_sems.at[base + slot], device)
        for slot, _, device in stage.peers()
    ]


def reduce_step(stage, rank, ref, landing, unit, send_sems, recv_sems, base):
    span = stage.held * unit
    first = rank // (stage.held * stage.radix) * (stage.radix * span)
    return [
        send(
            ref.at[pl.ds(first + other * span, span)],
            landing.at[slot],
            send_sems.at[base + slot],
            recv_sems.at[base + slot],
            device,
        )
        for slot, other, device in stage.peers()
    ]


def finish(copies):
    for copy in copies:
        copy.wait()


def normal(pre):
    return lax.rsqrt(jnp.sum(pre * pre, axis=-1, keepdims=True) + EPSILON)


def spread(values, lanes, columns):
    total = jnp.zeros((values.shape[0], LANES), values.dtype)
    for index in range(values.shape[1]):
        here_lane = lanes == columns[:, index : index + 1]
        total = total + jnp.where(here_lane, values[:, index : index + 1], 0)
    return total


def vector_rank(layout, owner, inner):
    bits = inner.bit_length() - 1
    parts = {"pb": owner >> bits, "pa": owner & (inner - 1)}
    rank = 0
    for axis, stride, radix, held in layout:
        digit = (parts[axis] >> (stride.bit_length() - 1)) & (radix - 1)
        rank = rank + digit * held
    return rank


def pair_row(pair, queries):
    return pair // queries * (2 * queries) + pair % queries


def step_kernel(
    layout,
    sizes,
    length_ref,
    query_length_ref,
    query_ref,
    head_ref,
    teacher_ref,
    owner_ref,
    local_ref,
    states_ref,
    score_ref,
    loss_ref,
    whole_ref,
    held_ref,
    pre_ref,
    query_pre_ref,
    passage_emb_ref,
    emb_ref,
    meta_ref,
    all_score_ref,
    turned_ref,
    table_ref,
    scalar_ref,
    ratio_ref,
    column_ref,
    query_part_ref,
    sent_ref,
    running_ref,
    total_ref,
    head_part_ref,
    head_sum_ref,
    cross_ref,
    *rest,
):
    outer, inner, parts = sizes
    count = len(layout)
    landings = rest[:count]
    head_landings = rest[count:-4]
    load_sems, table_sem, send_sems, recv_sems = rest[-4:]
    at = here()
    stages = [Stage(stage, at) for stage in layout]
    rank = rank_of(layout, at)
    length, passages, hidden = states_ref.shape
    queries, tokens, _ = query_ref.shape
    pairs = emb_ref.shape[0]
    width = head_ref.shape[1]
    rows = 2 * queries
    devices = pairs // queries
    step = length // parts
    span = step * passages

    loads = []
    for index in range(parts):
        part = pl.ds(index * step, step)
        load = pltpu.make_async_copy(states_ref.at[part], held_ref.at[part], load_sems.at[index])
        load.start()
        loads.append(load)
    barrier, greeted = greet(stages)

    for index in range(queries):
        pre = jnp.dot(query_ref[index], head_ref[...], preferred_element_type=F32)
        query_pre_ref[index] = pre
        emb_ref[rank * queries + index] = (pre * normal(pre)).astype(BF16)
    teacher = teacher_ref[...]
    target = teacher - jnp.log(jnp.sum(jnp.exp(teacher), axis=-1, keepdims=True))
    owner_rank = vector_rank(layout, owner_ref[...], inner)
    lanes = lax.broadcasted_iota(jnp.int32, (queries, LANES), 1)
    slot = lax.broadcasted_iota(jnp.int32, local_ref.shape, 0)
    code = local_ref[...]
    for index in range(queries):
        code = code + jnp.where(slot == index, query_length_ref[index] * passages, 0)
    meta_ref[rank, 0:queries, :] = spread(target, lanes, owner_rank)
    meta_ref[rank, queries:rows, :] = spread(code.astype(F32), lanes, owner_rank)
    pl.semaphore_wait(barrier, greeted)

    def project(index, carry):
        flat = held_ref[pl.ds(index * step, step)].reshape(span, hidden)
        pre_ref[pl.ds(pl.multiple_of(index * span, 8), span), :] = jnp.dot(
            flat, head_ref[...], preferred_element_type=F32
        )
        return carry

    def passage_pre(index):
        return pre_ref[pl.ds(index, length, stride=passages), :]

    def unit_rows(group, carry):
        for index in range(4):
            pre = passage_pre(group * 4 + index)
            passage_emb_ref[group * 4 + index] = (pre * normal(pre)).astype(BF16)
        return carry

    base = 0
    done = 0
    for number, stage in enumerate(stages):
        flight = gather_step(stage, rank, emb_ref, queries, send_sems, recv_sems, base)
        base += stage.radix - 1
        flight += gather_step(stage, rank, meta_ref, 1, send_sems, recv_sems, base)
        base += stage.radix - 1
        until = parts * (number + 1) // count
        for index in range(done, until):
            loads[index].wait()
            project(index, 0)
        done = until
        if number == count - 1:
            lax.fori_loop(0, passages // 4, unit_rows, 0)
        finish(flight)

    wide = devices * rows
    table = meta_ref[...].reshape(wide, LANES)
    turned = jnp.transpose(table)
    target = turned[:devices]
    column_code = jnp.sum(
        jnp.where(lax.broadcasted_iota(jnp.int32, table.shape, 1) == rank, table, 0.0),
        axis=1,
        keepdims=True,
    ).astype(jnp.int32)
    row_code = jnp.sum(
        jnp.where(lax.broadcasted_iota(jnp.int32, turned.shape, 0) == rank, turned, 0.0),
        axis=0,
        keepdims=True,
    ).astype(jnp.int32)
    low = passages.bit_length() - 1
    column_place = lax.broadcasted_iota(jnp.int32, (wide, 1), 0)
    row_place = lax.broadcasted_iota(jnp.int32, (1, wide), 1)
    column_valid = (column_place & (rows - 1)) >= queries
    row_valid = (row_place & (rows - 1)) >= queries
    column_local = jnp.where(column_valid, column_code & (passages - 1), passages)
    row_local = jnp.where(row_valid, row_code & (passages - 1), passages)
    column_key = column_local * wide + column_place
    row_key = row_local * wide + row_place
    place = jnp.sum((row_key < column_key).astype(jnp.int32), axis=1, keepdims=True)
    chosen = place == row_place
    pair_name = (column_place >> (rows.bit_length() - 1)) * queries + (
        column_place & (queries - 1)
    )
    table_ref[0:1, :] = row_code & (passages - 1)
    table_ref[1:2, :] = row_code >> low
    table_ref[2:3, :] = jnp.clip(
        jnp.sum(jnp.where(chosen, pair_name, 0), axis=0, keepdims=True), 0, pairs - 1
    )
    table_ref[3:4, :] = jnp.clip(
        jnp.sum((column_local <= row_place).astype(jnp.int32), axis=0, keepdims=True) - 1,
        0,
        pairs - 1,
    )
    table_ref[4:5, :] = jnp.sum(jnp.where(chosen, column_local, 0), axis=0, keepdims=True)
    to_scalar = pltpu.make_async_copy(table_ref, scalar_ref, table_sem)
    to_scalar.start()
    column_ref[...] = jnp.zeros_like(column_ref)
    to_scalar.wait()

    def local_of(pair):
        return scalar_ref[0, pair_row(pair, queries) + queries]

    def forward(group, carry):
        names = [group * queries + index for index in range(queries)]
        places = [local_of(name) for name in names]
        sim = jnp.concatenate(
            [
                lax.dot_general(
                    emb_ref[name],
                    passage_emb_ref[place],
                    (((1,), (1,)), ((), ())),
                    preferred_element_type=F32,
                )
                for name, place in zip(names, places)
            ],
            axis=0,
        )
        until = jnp.concatenate(
            [jnp.full((tokens, 1), length_ref[place], jnp.int32) for place in places], axis=0
        )
        alive = jnp.concatenate(
            [
                jnp.full((tokens, 1), scalar_ref[1, pair_row(name, queries) + queries], jnp.int32)
                for name in names
            ],
            axis=0,
        )
        exponent = jnp.where(
            lax.broadcasted_iota(jnp.int32, sim.shape, 1) < until, jnp.exp(sim / SOFTMAX_TEMP), 0.0
        )
        whole = jnp.sum(exponent, axis=-1, keepdims=True)
        live = (lax.broadcasted_iota(jnp.int32, whole.shape, 0) & (tokens - 1)) < alive
        ratio = (exponent * jnp.where(live, 1.0 / whole, 0.0)).astype(BF16)
        logs = jnp.where(live, SOFTMAX_TEMP * jnp.log(whole), 0.0)
        for index, name in enumerate(names):
            ratio_ref[name] = ratio[index * tokens : (index + 1) * tokens]
            column_ref[pl.ds(group * rows + index, 1), :] = jnp.broadcast_to(
                jnp.sum(logs[index * tokens : (index + 1) * tokens], axis=0, keepdims=True),
                (1, LANES),
            )
        return carry

    lax.fori_loop(0, devices, forward, 0, unroll=2)

    square = (LANES, LANES)
    diagonal = lax.broadcasted_iota(jnp.int32, square, 0) == lax.broadcasted_iota(
        jnp.int32, square, 1
    )
    blocks = wide // LANES
    all_score_ref[rank] = jnp.concatenate(
        [
            jnp.sum(
                jnp.where(diagonal, column_ref[block * LANES : (block + 1) * LANES], 0.0),
                axis=0,
                keepdims=True,
            )
            for block in range(blocks)
        ],
        axis=1,
    )

    def query_side(group, carry):
        names = [group * queries + index for index in range(queries)]
        found = [
            jnp.dot(ratio_ref[name], passage_emb_ref[local_of(name)], preferred_element_type=F32)
            for name in names
        ]
        for name, value in zip(names, found):
            query_part_ref[name] = value
        return carry

    done = 0
    for number, stage in enumerate(stages):
        flight = gather_step(stage, rank, all_score_ref, 1, send_sems, recv_sems, base)
        base += stage.radix - 1
        until = devices * (number + 1) // count
        lax.fori_loop(done, until, query_side, 0, unroll=2)
        done = until
        finish(flight)

    valid = (lax.broadcasted_iota(jnp.int32, (1, wide), 1) & (rows - 1)) < queries
    target = jnp.where(valid, target, 0.0)
    scores = jnp.where(valid, all_score_ref[...].reshape(devices, wide), 0.0)
    student = jnp.exp(scores)
    student_sum = jnp.sum(student, axis=0, keepdims=True)
    share = jnp.exp(target)
    mine = lax.broadcasted_iota(jnp.int32, scores.shape, 0) == rank
    weight = jnp.sum(
        jnp.where(mine, student / student_sum - share, 0.0), axis=0, keepdims=True
    )
    for block in range(blocks):
        upright = jnp.sum(
            jnp.where(
                diagonal,
                jnp.broadcast_to(weight[:, block * LANES : (block + 1) * LANES], square),
                0.0,
            ),
            axis=1,
            keepdims=True,
        )
        column_ref[block * LANES : (block + 1) * LANES] = jnp.broadcast_to(upright, square)

    def weight_of(pair):
        return column_ref[pl.ds(pair_row(pair, queries), 1), :]

    def scale(group, carry):
        for index in range(queries):
            pair = group * queries + index
            sent_ref[pair] = (query_part_ref[pair] * weight_of(pair)).astype(BF16)
        return carry

    lax.fori_loop(0, devices, scale, 0, unroll=2)

    bases = []
    for stage in stages:
        bases.append(base)
        base += stage.radix - 1

    def reduce_start(number):
        stage = stages[number]
        return reduce_step(
            stage, rank, sent_ref, landings[number], queries, send_sems, recv_sems, bases[number]
        )

    def reduce_end(number, flight):
        finish(flight)
        stage = stages[number]
        landing = landings[number]
        first = rank // stage.held * stage.held * queries

        def add(group, carry):
            for inner_index in range(queries):
                index = group * queries + inner_index
                value = sent_ref[first + index].astype(F32)
                for slot in range(stage.radix - 1):
                    value = value + landing[slot, index].astype(F32)
                if number:
                    sent_ref[first + index] = value.astype(BF16)
                else:
                    query_part_ref[index] = value
            return carry

        lax.fori_loop(0, stage.held, add, 0)

    def passage_side(group, carry):
        places = [group * 4 + index for index in range(4)]
        names = [scalar_ref[2, place] for place in places]
        found = [
            lax.dot_general(
                ratio_ref[name], emb_ref[name], (((0,), (0,)), ((), ())), preferred_element_type=F32
            )
            * weight_of(name)
            for name in names
        ]
        grown = total_ref[...]
        for place, value in zip(places, found):
            before = scalar_ref[4, jnp.maximum(place - 1, 0)]
            grown = grown * jnp.where(scalar_ref[4, place] == before, 1.0, 0.0) + value
            running_ref[place] = grown
        total_ref[...] = grown
        return carry

    def passage_grad(group, carry):
        for inner_index in range(4):
            index = group * 4 + inner_index
            last = scalar_ref[3, index]
            along = running_ref[last] * jnp.where(scalar_ref[4, last] == index, 1.0, 0.0)
            pre = passage_pre(index)
            inverse = normal(pre)
            unit = pre * inverse
            radial = jnp.sum(along * unit, axis=-1, keepdims=True)
            pre_ref[pl.ds(index, length, stride=passages), :] = (along - unit * radial) * inverse
        return carry

    def head_term(index, carry):
        head_sum_ref[...] += lax.dot_general(
            pre_ref[pl.ds(pl.multiple_of(index * span, 8), span), :].astype(BF16),
            held_ref[pl.ds(index * step, step)].reshape(span, hidden),
            (((0,), (0,)), ((), ())),
            preferred_element_type=F32,
        )
        return carry

    flight = reduce_start(count - 1)
    total_ref[...] = jnp.zeros_like(total_ref)
    head_sum_ref[...] = jnp.zeros_like(head_sum_ref)
    lax.fori_loop(0, pairs // 8, passage_side, 0)
    reduce_end(count - 1, flight)
    for number in range(count - 2, -1, -1):
        flight = reduce_start(number)
        if number == count - 2:
            lax.fori_loop(pairs // 8, pairs // 4, passage_side, 0)
            lax.fori_loop(0, passages // 4, passage_grad, 0)
        if number == 0:
            lax.fori_loop(0, parts, head_term, 0)
        reduce_end(number, flight)

    turned_ref[...] = jnp.zeros_like(turned_ref)
    turned_ref[:, 0:devices] = jnp.transpose(scores)
    own = turned_ref[pl.ds(pl.multiple_of(rank * rows, rows), rows), :][:queries]
    picked = jnp.zeros(owner_rank.shape, F32)
    for device in range(devices):
        picked = picked + jnp.where(owner_rank == device, own[:, device : device + 1], 0.0)
    score_ref[...] = picked
    loss = jnp.sum(
        jnp.sum(
            jnp.where(valid, share * (target - scores + jnp.log(student_sum)), 0.0),
            axis=0,
            keepdims=True,
        ),
        axis=1,
        keepdims=True,
    )
    loss_ref[...] = jnp.broadcast_to(loss / pairs, loss_ref.shape)

    for index in range(queries):
        along = query_part_ref[index]
        pre = query_pre_ref[index]
        inverse = normal(pre)
        unit = pre * inverse
        radial = jnp.sum(along * unit, axis=-1, keepdims=True)
        grad = ((along - unit * radial) * inverse).astype(BF16)
        head_sum_ref[...] += lax.dot_general(
            grad, query_ref[index], (((0,), (0,)), ((), ())), preferred_element_type=F32
        )

    chunks, rows_each, _ = head_part_ref.shape
    upright = jnp.transpose(head_sum_ref[...])
    for index in range(chunks):
        head_part_ref[index] = upright[index * rows_each : (index + 1) * rows_each].astype(BF16)

    outer_count = count - len(head_landings)
    chunk = rank // outer
    for number in range(count - 1, outer_count - 1, -1):
        stage = stages[number]
        landing = head_landings[number - outer_count]
        held = stage.held // outer
        first = chunk // (held * stage.radix) * (held * stage.radix)
        flight = [
            send(
                head_part_ref.at[pl.ds(first + other * held, held)],
                landing.at[slot],
                send_sems.at[base + slot],
                recv_sems.at[base + slot],
                device,
            )
            for slot, other, device in stage.peers()
        ]
        base += stage.radix - 1
        finish(flight)
        own = chunk // held * held
        for index in range(held):
            value = head_part_ref[own + index].astype(F32)
            for slot in range(stage.radix - 1):
                value = value + landing[slot, index].astype(F32)
            head_part_ref[own + index] = value.astype(BF16)

    place = 0
    for number in range(outer_count):
        stage = stages[number]
        cross_ref[place + stage.digit] = head_part_ref[chunk]
        flight = [
            send(
                cross_ref.at[place + stage.digit],
                cross_ref.at[place + stage.digit],
                send_sems.at[base + slot],
                recv_sems.at[base + slot],
                device,
            )
            for slot, _, device in stage.peers()
        ]
        base += stage.radix - 1
        finish(flight)
        value = cross_ref[place].astype(F32)
        for digit in range(1, stage.radix):
            value = value + cross_ref[place + digit].astype(F32)
        head_part_ref[chunk] = value.astype(BF16)
        place += stage.radix

    whole_ref[chunk] = head_part_ref[chunk]
    for number in range(outer_count, count):
        stage = stages[number]
        held = stage.held // outer
        block = whole_ref.at[pl.ds(chunk // held * held, held)]
        flight = [
            send(block, block, send_sems.at[base + slot], recv_sems.at[base + slot], device)
            for slot, _, device in stage.peers()
        ]
        base += stage.radix - 1
        finish(flight)


def on_device_dense(
    query_states,
    passage_states,
    head,
    teacher,
    cand_owner,
    cand_local,
    query_lengths,
    passage_lengths,
):
    outer = lax.axis_size("pb")
    inner = lax.axis_size("pa")
    devices = outer * inner
    queries, tokens, hidden = query_states.shape
    passages, length, _ = passage_states.shape
    width = head.shape[1]
    pairs = queries * devices
    wide = 2 * pairs
    layout = exchange_stages(outer, inner)
    peers = sum(stage[2] - 1 for stage in layout)
    parts = 10 if length % 10 == 0 else 1

    vmem = pl.BlockSpec(memory_space=pltpu.VMEM)
    smem = pl.BlockSpec(memory_space=pltpu.SMEM)
    anywhere = pl.BlockSpec(memory_space=pl.ANY)
    landings = [
        pltpu.VMEM((radix - 1, held * queries, tokens, width), BF16)
        for _, _, radix, held in layout
    ]
    chunks = inner
    rows_each = hidden // chunks
    head_landings = [
        pltpu.VMEM((radix - 1, held // outer, rows_each, width), BF16)
        for axis, _, radix, held in layout
        if axis == "pa"
    ]
    cross = sum(stage[2] for stage in layout if stage[0] == "pb")
    scores, loss, head_grad = pl.pallas_call(
        functools.partial(step_kernel, layout, (outer, inner, parts)),
        out_shape=[
            jax.ShapeDtypeStruct(teacher.shape, F32),
            jax.ShapeDtypeStruct((8, LANES), F32),
            jax.ShapeDtypeStruct((chunks, rows_each, width), BF16),
        ],
        in_specs=[smem, smem, vmem, vmem, vmem, vmem, vmem, anywhere],
        out_specs=[vmem] * 3,
        scratch_shapes=[
            pltpu.VMEM((length, passages, hidden), BF16),
            pltpu.VMEM(((length + 1) * passages, width), F32),
            pltpu.VMEM((queries, tokens, width), F32),
            pltpu.VMEM((passages, length, width), BF16),
            pltpu.VMEM((pairs, tokens, width), BF16),
            pltpu.VMEM((devices, 2 * queries, LANES), F32),
            pltpu.VMEM((devices, 1, wide), F32),
            pltpu.VMEM((wide, LANES), F32),
            pltpu.VMEM((8, wide), jnp.int32),
            pltpu.SMEM((8, wide), jnp.int32),
            pltpu.VMEM((pairs, tokens, length), BF16),
            pltpu.VMEM((wide, LANES), F32),
            pltpu.VMEM((pairs, tokens, width), F32),
            pltpu.VMEM((pairs, tokens, width), BF16),
            pltpu.VMEM((pairs, length, width), F32),
            pltpu.VMEM((length, width), F32),
            pltpu.VMEM((chunks, rows_each, width), BF16),
            pltpu.VMEM((width, hidden), F32),
            pltpu.VMEM((cross, rows_each, width), BF16),
            *landings,
            *head_landings,
            pltpu.SemaphoreType.DMA((parts,)),
            pltpu.SemaphoreType.DMA,
            pltpu.SemaphoreType.DMA((6 * peers,)),
            pltpu.SemaphoreType.DMA((6 * peers,)),
        ],
        compiler_params=pltpu.CompilerParams(
            collective_id=0, has_side_effects=True, vmem_limit_bytes=56 * 2**20
        ),
    )(
        passage_lengths,
        query_lengths,
        query_states,
        head,
        teacher,
        cand_owner,
        cand_local,
        jnp.transpose(passage_states, (1, 0, 2)),
    )
    return (scores, loss[0, 0], head_grad.astype(F32).reshape(hidden, width))


def suits_dense(mesh, arguments):
    outer, inner = mesh.shape["pb"], mesh.shape["pa"]
    devices = outer * inner
    queries = arguments[0].shape[0]
    hidden = arguments[0].shape[2]
    return (
        arguments[4].shape[1] == devices
        and queries == LANES
        and queries // devices == 4
        and outer & (outer - 1) == 0
        and inner & (inner - 1) == 0
        and hidden % (16 * inner) == 0
        and arguments[0].shape[1] == 32
        and arguments[1].shape[0] // devices in (16, 32, 64)
        and arguments[1].shape[1] * (arguments[1].shape[0] // devices) % 8 == 0
        and arguments[2].shape[1] == LANES
    )


def solution(mesh):
    def run(*arguments):
        body = on_device_dense if suits_dense(mesh, arguments) else on_device
        return placed(mesh, body)(*arguments)

    return run


def placed(mesh, body):
    return jax.shard_map(
        body,
        mesh=mesh,
        in_specs=(
            P(("pb", "pa"), None, None),
            P(("pb", "pa"), None, None),
            P(),
            P(("pb", "pa"), None),
            P(("pb", "pa"), None),
            P(("pb", "pa"), None),
            P(("pb", "pa")),
            P(("pb", "pa")),
        ),
        out_specs=(P(("pb", "pa"), None), P(), P()),
        check_vma=False,
    )
```

profile of v0, /device:TPU:0, one launch (start us, length us, event | category | flops | bytes accessed | tf_op | source)
XLA Modules:
  0.0 81.7 jit_solution(14017130666439882997)
XLA Ops:
  0.6 76.9 %shard_map.103 = (f32[4,32]{1,0:T(4,128)}, f32[8,128]{1,0:T(8,128)}, bf16[8,96,128]{2,1,0:T(8,128)(2,1)}) custom-call(s32[32]{0:T(128)} %length_ref.1, s32[4]{0:T(128)} %query_length_ref.1, bf16[4,32,768]{2,1,0:T(8,128)(2,1)} %query_ref.1, bf16[768,128]{1,0:T(8,128)(2,1)} %head_ref.1, f32[4,32]{1,0:T(4,128)} %teacher_ref.1, s32[4,32]{1,0:T(4,128)} %owner_ref.1, ...), custom_call_target="tpu_custom_call" | custom-call | tf_op jit(solution)/shard_map/pallas_call | solution.py:820
  77.5 1.2 %slice.3 = f32[1,1]{1,0:T(1,128)} slice(f32[8,128]{1,0:T(8,128)} %get-tuple-element.7), slice={[0:1], [0:1]} | slice | bytes 8 | tf_op jit(solution)/shard_map/slice | solution.py:869
  78.7 1.7 %bitcast_convert_fusion = f32[768,128]{1,0:T(8,128)} fusion(bf16[8,96,128]{2,1,0:T(8,128)(2,1)} %get-tuple-element.8), kind=kLoop, calls=%fused_computation | loop fusion | flops 98304 | bytes 589824 | tf_op jit(solution)/shard_map/reshape | solution.py:869
  80.4 1.2 %copy.12 = f32[4,32]{1,0:T(4,128)} copy(f32[4,32]{1,0:T(4,128)} %get-tuple-element.12) | data formatting | bytes 1024
where the time goes:
time: 81.9 us; the launch traced here: 81.7 us
  Pallas kernels  76.9 us (94%)
  local copies, waits for them, and re-layouts  2.41 us (3%)
  other arithmetic  1.7 us (2%)
    pallas_call x1, Pallas kernels, on_device_dense(): pl.pallas_call(functools.partial(step_kernel, layout, (outer, inner, part...  76.9 us
    reshape x1, other arithmetic, on_device_dense(): return (scores, loss[0, 0], head_grad.astype(F32).reshape(hidden, width))  1.7 us

commit v1 on v0

--- a/solution.py
+++ b/solution.py
@@ -257,6 +257,21 @@
         return found
 
 
+class Plane:
+    def __init__(self, at, outer, inner):
+        self.at = at
+        self.held = outer
+        self.radix = inner
+        self.digit = at["pa"]
+
+    def peers(self):
+        found = []
+        for step in range(1, self.radix):
+            other = (self.digit + step) % self.radix
+            found.append((step - 1, other, (self.at["pb"], other)))
+        return found
+
+
 def greet(stages):
     barrier = pltpu.get_barrier_semaphore()
     count = 0
@@ -364,7 +379,6 @@
     query_part_ref,
     sent_ref,
     running_ref,
-    total_ref,
     head_part_ref,
     head_sum_ref,
     cross_ref,
@@ -373,7 +387,7 @@
     outer, inner, parts = sizes
     count = len(layout)
     landings = rest[:count]
-    head_landings = rest[count:-4]
+    head_landing = rest[count]
     load_sems, table_sem, send_sems, recv_sems = rest[-4:]
     at = here()
     stages = [Stage(stage, at) for stage in layout]
@@ -393,7 +407,10 @@
         load = pltpu.make_async_copy(states_ref.at[part], held_ref.at[part], load_sems.at[index])
         load.start()
         loads.append(load)
-    barrier, greeted = greet(stages)
+    plane = Plane(at, outer, inner)
+    outer_stages = [stage for stage in stages if stage.axis == "pb"]
+    short_stages = outer_stages + [plane]
+    barrier, greeted = greet(short_stages)
 
     for index in range(queries):
         pre = jnp.dot(query_ref[index], head_ref[...], preferred_element_type=F32)
@@ -427,21 +444,39 @@
             passage_emb_ref[group * 4 + index] = (pre * normal(pre)).astype(BF16)
         return carry
 
+    emb_bases = []
     base = 0
-    done = 0
-    for number, stage in enumerate(stages):
-        flight = gather_step(stage, rank, emb_ref, queries, send_sems, recv_sems, base)
+    for stage in stages:
+        emb_bases.append(base)
         base += stage.radix - 1
-        flight += gather_step(stage, rank, meta_ref, 1, send_sems, recv_sems, base)
-        base += stage.radix - 1
-        until = parts * (number + 1) // count
-        for index in range(done, until):
+
+    def gather_emb(number):
+        return gather_step(
+            stages[number], rank, emb_ref, queries, send_sems, recv_sems, emb_bases[number]
+        )
+
+    def project_until(first, until):
+        for index in range(first, until):
             loads[index].wait()
             project(index, 0)
+
+    done = 0
+    flight = gather_emb(0)
+    for number, stage in enumerate(short_stages):
+        meta_flight = gather_step(stage, rank, meta_ref, 1, send_sems, recv_sems, base)
+        base += stage.radix - 1
+        until = parts * 2 * (number + 1) // (5 * len(short_stages))
+        project_until(done, until)
         done = until
-        if number == count - 1:
-            lax.fori_loop(0, passages // 4, unit_rows, 0)
+        finish(meta_flight)
+    for number in range(1, count - 1):
         finish(flight)
+        flight = gather_emb(number)
+        until = parts * (number + 1) // (count - 1) if number < count - 2 else parts
+        project_until(done, until)
+        done = until
+    project_until(done, parts)
+    lax.fori_loop(0, passages // 4, unit_rows, 0, unroll=2)
 
     wide = devices * rows
     table = meta_ref[...].reshape(wide, LANES)
@@ -516,7 +551,7 @@
             axis=0,
         )
         exponent = jnp.where(
-            lax.broadcasted_iota(jnp.int32, sim.shape, 1) < until, jnp.exp(sim / SOFTMAX_TEMP), 0.0
+            lax.broadcasted_iota(jnp.int32, sim.shape, 1) < until, jnp.exp(sim * (1.0 / SOFTMAX_TEMP)), 0.0
         )
         whole = jnp.sum(exponent, axis=-1, keepdims=True)
         live = (lax.broadcasted_iota(jnp.int32, whole.shape, 0) & (tokens - 1)) < alive
@@ -530,7 +565,20 @@
             )
         return carry
 
-    lax.fori_loop(0, devices, forward, 0, unroll=2)
+    finish(flight)
+    flight = gather_emb(count - 1)
+    top = stages[count - 1]
+    near = rank // top.held * top.held
+
+    def forward_near(group, carry):
+        return forward(near + group, carry)
+
+    def forward_far(group, carry):
+        return forward((near + top.held + group) % devices, carry)
+
+    lax.fori_loop(0, top.held, forward_near, 0, unroll=4)
+    finish(flight)
+    lax.fori_loop(0, devices - top.held, forward_far, 0, unroll=4)
 
     square = (LANES, LANES)
     diagonal = lax.broadcasted_iota(jnp.int32, square, 0) == lax.broadcasted_iota(
@@ -560,10 +608,10 @@
         return carry
 
     done = 0
-    for number, stage in enumerate(stages):
+    for number, stage in enumerate(short_stages):
         flight = gather_step(stage, rank, all_score_ref, 1, send_sems, recv_sems, base)
         base += stage.radix - 1
-        until = devices * (number + 1) // count
+        until = devices * (number + 1) // len(short_stages)
         lax.fori_loop(done, until, query_side, 0, unroll=2)
         done = until
         finish(flight)
@@ -642,24 +690,26 @@
             * weight_of(name)
             for name in names
         ]
-        grown = total_ref[...]
+        grown = carry
         for place, value in zip(places, found):
             before = scalar_ref[4, jnp.maximum(place - 1, 0)]
             grown = grown * jnp.where(scalar_ref[4, place] == before, 1.0, 0.0) + value
             running_ref[place] = grown
-        total_ref[...] = grown
-        return carry
+        return grown
 
     def passage_grad(group, carry):
-        for inner_index in range(4):
-            index = group * 4 + inner_index
+        indices = [group * 4 + index for index in range(4)]
+        found = []
+        for index in indices:
             last = scalar_ref[3, index]
             along = running_ref[last] * jnp.where(scalar_ref[4, last] == index, 1.0, 0.0)
             pre = passage_pre(index)
             inverse = normal(pre)
             unit = pre * inverse
             radial = jnp.sum(along * unit, axis=-1, keepdims=True)
-            pre_ref[pl.ds(index, length, stride=passages), :] = (along - unit * radial) * inverse
+            found.append((along - unit * radial) * inverse)
+        for index, value in zip(indices, found):
+            pre_ref[pl.ds(index, length, stride=passages), :] = value
         return carry
 
     def head_term(index, carry):
@@ -672,18 +722,48 @@
         return carry
 
     flight = reduce_start(count - 1)
-    total_ref[...] = jnp.zeros_like(total_ref)
     head_sum_ref[...] = jnp.zeros_like(head_sum_ref)
-    lax.fori_loop(0, pairs // 8, passage_side, 0)
+    total = lax.fori_loop(
+        0, pairs // 8, passage_side, jnp.zeros((length, width), F32), unroll=2
+    )
     reduce_end(count - 1, flight)
     for number in range(count - 2, -1, -1):
         flight = reduce_start(number)
         if number == count - 2:
-            lax.fori_loop(pairs // 8, pairs // 4, passage_side, 0)
+            lax.fori_loop(pairs // 8, pairs // 4, passage_side, total, unroll=2)
             lax.fori_loop(0, passages // 4, passage_grad, 0)
         if number == 0:
             lax.fori_loop(0, parts, head_term, 0)
         reduce_end(number, flight)
+
+    for index in range(queries):
+        along = query_part_ref[index]
+        pre = query_pre_ref[index]
+        inverse = normal(pre)
+        unit = pre * inverse
+        radial = jnp.sum(along * unit, axis=-1, keepdims=True)
+        grad = ((along - unit * radial) * inverse).astype(BF16)
+        head_sum_ref[...] += lax.dot_general(
+            grad, query_ref[index], (((0,), (0,)), ((), ())), preferred_element_type=F32
+        )
+
+    chunks, rows_each, _ = head_part_ref.shape
+    upright = jnp.transpose(head_sum_ref[...])
+    for index in range(chunks):
+        head_part_ref[index] = upright[index * rows_each : (index + 1) * rows_each].astype(BF16)
+
+    chunk = at["pa"]
+    flight = [
+        send(
+            head_part_ref.at[other],
+            head_landing.at[slot],
+            send_sems.at[base + slot],
+            recv_sems.at[base + slot],
+            device,
+        )
+        for slot, other, device in plane.peers()
+    ]
+    base += inner - 1
 
     turned_ref[...] = jnp.zeros_like(turned_ref)
     turned_ref[:, 0:devices] = jnp.transpose(scores)
@@ -701,62 +781,19 @@
         axis=1,
         keepdims=True,
     )
-    loss_ref[...] = jnp.broadcast_to(loss / pairs, loss_ref.shape)
-
-    for index in range(queries):
-        along = query_part_ref[index]
-        pre = query_pre_ref[index]
-        inverse = normal(pre)
-        unit = pre * inverse
-        radial = jnp.sum(along * unit, axis=-1, keepdims=True)
-        grad = ((along - unit * radial) * inverse).astype(BF16)
-        head_sum_ref[...] += lax.dot_general(
-            grad, query_ref[index], (((0,), (0,)), ((), ())), preferred_element_type=F32
-        )
-
-    chunks, rows_each, _ = head_part_ref.shape
-    upright = jnp.transpose(head_sum_ref[...])
-    for index in range(chunks):
-        head_part_ref[index] = upright[index * rows_each : (index + 1) * rows_each].astype(BF16)
-
-    outer_count = count - len(head_landings)
-    chunk = rank // outer
-    for number in range(count - 1, outer_count - 1, -1):
-        stage = stages[number]
-        landing = head_landings[number - outer_count]
-        held = stage.held // outer
-        first = chunk // (held * stage.radix) * (held * stage.radix)
+    loss_ref[0, 0] = (loss / pairs)[0, 0]
+
+    finish(flight)
+    value = head_part_ref[chunk].astype(F32)
+    for slot in range(inner - 1):
+        value = value + head_landing[slot].astype(F32)
+
+    place = 0
+    for stage in outer_stages:
+        cross_ref[place + stage.digit] = value.astype(BF16)
+        part = cross_ref.at[place + stage.digit]
         flight = [
-            send(
-                head_part_ref.at[pl.ds(first + other * held, held)],
-                landing.at[slot],
-                send_sems.at[base + slot],
-                recv_sems.at[base + slot],
-                device,
-            )
-            for slot, other, device in stage.peers()
-        ]
-        base += stage.radix - 1
-        finish(flight)
-        own = chunk // held * held
-        for index in range(held):
-            value = head_part_ref[own + index].astype(F32)
-            for slot in range(stage.radix - 1):
-                value = value + landing[slot, index].astype(F32)
-            head_part_ref[own + index] = value.astype(BF16)
-
-    place = 0
-    for number in range(outer_count):
-        stage = stages[number]
-        cross_ref[place + stage.digit] = head_part_ref[chunk]
-        flight = [
-            send(
-                cross_ref.at[place + stage.digit],
-                cross_ref.at[place + stage.digit],
-                send_sems.at[base + slot],
-                recv_sems.at[base + slot],
-                device,
-            )
+            send(part, part, send_sems.at[base + slot], recv_sems.at[base + slot], device)
             for slot, _, device in stage.peers()
         ]
         base += stage.radix - 1
@@ -764,20 +801,15 @@
         value = cross_ref[place].astype(F32)
         for digit in range(1, stage.radix):
             value = value + cross_ref[place + digit].astype(F32)
-        head_part_ref[chunk] = value.astype(BF16)
         place += stage.radix
 
-    whole_ref[chunk] = head_part_ref[chunk]
-    for number in range(outer_count, count):
-        stage = stages[number]
-        held = stage.held // outer
-        block = whole_ref.at[pl.ds(chunk // held * held, held)]
-        flight = [
-            send(block, block, send_sems.at[base + slot], recv_sems.at[base + slot], device)
-            for slot, _, device in stage.peers()
-        ]
-        base += stage.radix - 1
-        finish(flight)
+    whole_ref[chunk] = value.astype(BF16)
+    part = whole_ref.at[chunk]
+    flight = [
+        send(part, part, send_sems.at[base + slot], recv_sems.at[base + slot], device)
+        for slot, _, device in plane.peers()
+    ]
+    finish(flight)
 
 
 def on_device_dense(
@@ -799,7 +831,7 @@
     pairs = queries * devices
     wide = 2 * pairs
     layout = exchange_stages(outer, inner)
-    peers = sum(stage[2] - 1 for stage in layout)
+    peers = outer + inner
     parts = 10 if length % 10 == 0 else 1
 
     vmem = pl.BlockSpec(memory_space=pltpu.VMEM)
@@ -811,21 +843,16 @@
     ]
     chunks = inner
     rows_each = hidden // chunks
-    head_landings = [
-        pltpu.VMEM((radix - 1, held // outer, rows_each, width), BF16)
-        for axis, _, radix, held in layout
-        if axis == "pa"
-    ]
     cross = sum(stage[2] for stage in layout if stage[0] == "pb")
     scores, loss, head_grad = pl.pallas_call(
         functools.partial(step_kernel, layout, (outer, inner, parts)),
         out_shape=[
             jax.ShapeDtypeStruct(teacher.shape, F32),
-            jax.ShapeDtypeStruct((8, LANES), F32),
+            jax.ShapeDtypeStruct((1, 1), F32),
             jax.ShapeDtypeStruct((chunks, rows_each, width), BF16),
         ],
         in_specs=[smem, smem, vmem, vmem, vmem, vmem, vmem, anywhere],
-        out_specs=[vmem] * 3,
+        out_specs=[vmem, smem, vmem],
         scratch_shapes=[
             pltpu.VMEM((length, passages, hidden), BF16),
             pltpu.VMEM(((length + 1) * passages, width), F32),
@@ -842,12 +869,11 @@
             pltpu.VMEM((pairs, tokens, width), F32),
             pltpu.VMEM((pairs, tokens, width), BF16),
             pltpu.VMEM((pairs, length, width), F32),
-            pltpu.VMEM((length, width), F32),
             pltpu.VMEM((chunks, rows_each, width), BF16),
             pltpu.VMEM((width, hidden), F32),
             pltpu.VMEM((cross, rows_each, width), BF16),
             *landings,
-            *head_landings,
+            pltpu.VMEM((inner - 1, rows_each, width), BF16),
             pltpu.SemaphoreType.DMA((parts,)),
             pltpu.SemaphoreType.DMA,
             pltpu.SemaphoreType.DMA((6 * peers,)),
@@ -866,7 +892,7 @@
         cand_local,
         jnp.transpose(passage_states, (1, 0, 2)),
     )
-    return (scores, loss[0, 0], head_grad.astype(F32).reshape(hidden, width))
+    return (scores, loss.reshape(()), head_grad.astype(F32).reshape(hidden, width))
 
 
 def suits_dense(mesh, arguments):

time: 81.9 us -> 72.9 us (0.89)
  Pallas kernels: 76.9 us -> 67.4 us
  between operations: 0.64 us -> 2.33 us
  local copies, waits for them, and re-layouts: 2.41 us -> 1.23 us
    pallas_call x1, Pallas kernels: 76.9 us -> 67.4 us  [on_device_dense(): pl.pallas_call(functools.partial(step_kernel, layout, (outer, inner, part...]
    slice x1 -> x0, local copies, waits for them, and re-layouts: 1.18 us -> none  [on_device_dense(): return (scores, loss[0, 0], head_grad.astype(F32).reshape(hidden, width))]
where the time goes in v1:
time: 72.9 us; the launch traced here: 72.7 us
  Pallas kernels  67.4 us (92%)
  between operations  2.33 us (3%)
  other arithmetic  1.7 us (2%)
  local copies, waits for them, and re-layouts  1.23 us (2%)
    pallas_call x1, Pallas kernels, on_device_dense(): pl.pallas_call(functools.partial(step_kernel, layout, (outer, inner, part...  67.4 us
    reshape x1, other arithmetic, on_device_dense(): head_grad.astype(F32).reshape(hidden, width)  1.7 us

profile of v1, /device:TPU:0, one launch (start us, length us, event | category | flops | bytes accessed | tf_op | source)
XLA Modules:
  0.0 72.7 jit_solution(17471536461117148452)
XLA Ops:
  0.6 67.4 %shard_map.103 = (f32[4,32]{1,0:T(4,128)}, f32[1,1]{1,0:T(1,128)}, bf16[8,96,128]{2,1,0:T(8,128)(2,1)}) custom-call(s32[32]{0:T(128)} %length_ref.1, s32[4]{0:T(128)} %query_length_ref.1, bf16[4,32,768]{2,1,0:T(8,128)(2,1)} %query_ref.1, bf16[768,128]{1,0:T(8,128)(2,1)} %head_ref.1, f32[4,32]{1,0:T(4,128)} %teacher_ref.1, s32[4,32]{1,0:T(4,128)} %owner_ref.1, ...), custom_call_target="tpu_custom_call" | custom-call | tf_op jit(solution)/shard_map/pallas_call | solution.py:847
  68.1 1.7 %bitcast_convert_fusion = f32[768,128]{1,0:T(8,128)} fusion(bf16[8,96,128]{2,1,0:T(8,128)(2,1)} %get-tuple-element.8), kind=kLoop, calls=%fused_computation | loop fusion | flops 98304 | bytes 589824 | tf_op jit(solution)/shard_map/reshape | solution.py:895
  69.8 1.2 %copy.13 = f32[4,32]{1,0:T(4,128)} copy(f32[4,32]{1,0:T(4,128)} %get-tuple-element.12) | data formatting | bytes 1024

commit v2 on v1

--- a/solution.py
+++ b/solution.py
@@ -368,6 +368,9 @@
     pre_ref,
     query_pre_ref,
     passage_emb_ref,
+    unit_ref,
+    inverse_ref,
+    upright_ref,
     emb_ref,
     meta_ref,
     all_score_ref,
@@ -441,7 +444,11 @@
     def unit_rows(group, carry):
         for index in range(4):
             pre = passage_pre(group * 4 + index)
-            passage_emb_ref[group * 4 + index] = (pre * normal(pre)).astype(BF16)
+            inverse = normal(pre)
+            unit = pre * inverse
+            passage_emb_ref[group * 4 + index] = unit.astype(BF16)
+            unit_ref[group * 4 + index] = unit
+            inverse_ref[group * 4 + index] = jnp.broadcast_to(inverse, unit.shape)
         return carry
 
     emb_bases = []
@@ -565,18 +572,24 @@
             )
         return carry
 
+    top = stages[count - 1]
+    near = rank // top.held * top.held
+    first_held = stages[count - 2].held
+    nearest = rank // first_held * first_held
+
+    def forward_nearest(group, carry):
+        return forward(nearest + group, carry)
+
+    def forward_near(group, carry):
+        return forward(near + (nearest - near + first_held + group) % top.held, carry)
+
+    def forward_far(group, carry):
+        return forward((near + top.held + group) % devices, carry)
+
+    lax.fori_loop(0, first_held, forward_nearest, 0, unroll=4)
     finish(flight)
     flight = gather_emb(count - 1)
-    top = stages[count - 1]
-    near = rank // top.held * top.held
-
-    def forward_near(group, carry):
-        return forward(near + group, carry)
-
-    def forward_far(group, carry):
-        return forward((near + top.held + group) % devices, carry)
-
-    lax.fori_loop(0, top.held, forward_near, 0, unroll=4)
+    lax.fori_loop(0, top.held - first_held, forward_near, 0, unroll=4)
     finish(flight)
     lax.fori_loop(0, devices - top.held, forward_far, 0, unroll=4)
 
@@ -603,8 +616,12 @@
             jnp.dot(ratio_ref[name], passage_emb_ref[local_of(name)], preferred_element_type=F32)
             for name in names
         ]
+        turned_ratio = jnp.transpose(
+            ratio_ref[pl.ds(group * queries, queries)].reshape(queries * tokens, length)
+        )
         for name, value in zip(names, found):
             query_part_ref[name] = value
+        upright_ref[group] = turned_ratio
         return carry
 
     done = 0
@@ -612,7 +629,7 @@
         flight = gather_step(stage, rank, all_score_ref, 1, send_sems, recv_sems, base)
         base += stage.radix - 1
         until = devices * (number + 1) // len(short_stages)
-        lax.fori_loop(done, until, query_side, 0, unroll=2)
+        lax.fori_loop(done, until, query_side, 0, unroll=4)
         done = until
         finish(flight)
 
@@ -647,7 +664,13 @@
             sent_ref[pair] = (query_part_ref[pair] * weight_of(pair)).astype(BF16)
         return carry
 
-    lax.fori_loop(0, devices, scale, 0, unroll=2)
+    def scale_far(group, carry):
+        return scale((near + top.held + group) % devices, carry)
+
+    def scale_near(group, carry):
+        return scale(near + group, carry)
+
+    lax.fori_loop(0, devices - top.held, scale_far, 0, unroll=4)
 
     bases = []
     for stage in stages:
@@ -680,13 +703,21 @@
 
         lax.fori_loop(0, stage.held, add, 0)
 
+    def placed_rows(name):
+        held = emb_ref[name].astype(F32)
+        return jnp.concatenate(
+            [
+                held * jnp.where(name % queries == index, 1.0, 0.0)
+                for index in range(queries)
+            ],
+            axis=0,
+        ).astype(BF16)
+
     def passage_side(group, carry):
         places = [group * 4 + index for index in range(4)]
         names = [scalar_ref[2, place] for place in places]
         found = [
-            lax.dot_general(
-                ratio_ref[name], emb_ref[name], (((0,), (0,)), ((), ())), preferred_element_type=F32
-            )
+            jnp.dot(upright_ref[name // queries], placed_rows(name), preferred_element_type=F32)
             * weight_of(name)
             for name in names
         ]
@@ -703,11 +734,9 @@
         for index in indices:
             last = scalar_ref[3, index]
             along = running_ref[last] * jnp.where(scalar_ref[4, last] == index, 1.0, 0.0)
-            pre = passage_pre(index)
-            inverse = normal(pre)
-            unit = pre * inverse
+            unit = unit_ref[index]
             radial = jnp.sum(along * unit, axis=-1, keepdims=True)
-            found.append((along - unit * radial) * inverse)
+            found.append((along - unit * radial) * inverse_ref[index])
         for index, value in zip(indices, found):
             pre_ref[pl.ds(index, length, stride=passages), :] = value
         return carry
@@ -722,16 +751,17 @@
         return carry
 
     flight = reduce_start(count - 1)
+    lax.fori_loop(0, top.held, scale_near, 0, unroll=4)
     head_sum_ref[...] = jnp.zeros_like(head_sum_ref)
     total = lax.fori_loop(
-        0, pairs // 8, passage_side, jnp.zeros((length, width), F32), unroll=2
+        0, pairs // 8, passage_side, jnp.zeros((length, width), F32), unroll=4
     )
     reduce_end(count - 1, flight)
     for number in range(count - 2, -1, -1):
         flight = reduce_start(number)
         if number == count - 2:
-            lax.fori_loop(pairs // 8, pairs // 4, passage_side, total, unroll=2)
-            lax.fori_loop(0, passages // 4, passage_grad, 0)
+            lax.fori_loop(pairs // 8, pairs // 4, passage_side, total, unroll=4)
+            lax.fori_loop(0, passages // 4, passage_grad, 0, unroll=2)
         if number == 0:
             lax.fori_loop(0, parts, head_term, 0)
         reduce_end(number, flight)
@@ -810,6 +840,14 @@
         for slot, _, device in plane.peers()
     ]
     finish(flight)
+
+
+def widen_kernel(narrow_ref, picked_ref, sum_ref, wide_ref, score_ref, loss_ref):
+    rows_each = narrow_ref.shape[1]
+    for index in range(narrow_ref.shape[0]):
+        wide_ref[index * rows_each : (index + 1) * rows_each, :] = narrow_ref[index].astype(F32)
+    score_ref[...] = picked_ref[...]
+    loss_ref[0, 0] = sum_ref[0, 0]
 
 
 def on_device_dense(
@@ -858,6 +896,9 @@
             pltpu.VMEM(((length + 1) * passages, width), F32),
             pltpu.VMEM((queries, tokens, width), F32),
             pltpu.VMEM((passages, length, width), BF16),
+            pltpu.VMEM((passages, length, width), F32),
+            pltpu.VMEM((passages, length, width), F32),
+            pltpu.VMEM((devices, length, queries * tokens), BF16),
             pltpu.VMEM((pairs, tokens, width), BF16),
             pltpu.VMEM((devices, 2 * queries, LANES), F32),
             pltpu.VMEM((devices, 1, wide), F32),
@@ -892,7 +933,17 @@
         cand_local,
         jnp.transpose(passage_states, (1, 0, 2)),
     )
-    return (scores, loss.reshape(()), head_grad.astype(F32).reshape(hidden, width))
+    head_grad, scores, loss = pl.pallas_call(
+        widen_kernel,
+        out_shape=[
+            jax.ShapeDtypeStruct((hidden, width), F32),
+            jax.ShapeDtypeStruct(teacher.shape, F32),
+            jax.ShapeDtypeStruct((1, 1), F32),
+        ],
+        in_specs=[vmem, vmem, smem],
+        out_specs=[vmem, vmem, smem],
+    )(head_grad, scores, loss)
+    return (scores, loss.reshape(()), head_grad)
 
 
 def suits_dense(mesh, arguments):

time: 72.9 us -> 68.4 us (0.938)
  other arithmetic: 1.7 us -> 0 us
  between operations: 2.33 us -> 0.64 us
  local copies, waits for them, and re-layouts: 1.23 us -> 0 us
    pallas_call x0 -> x1, Pallas kernels: none -> 2.34 us  [on_device_dense(): pl.pallas_call(widen_kernel, out_shape=[jax.ShapeDtypeStruct((hidden, wid...]
    pallas_call x1, Pallas kernels: 67.4 us -> 65.3 us  [on_device_dense(): pl.pallas_call(functools.partial(step_kernel, layout, (outer, inner, part...]
    reshape x1 -> x0, other arithmetic: 1.7 us -> none  [on_device_dense(): head_grad.astype(F32).reshape(hidden, width)]
    unnamed x1 -> x0, local copies, waits for them, and re-layouts: 1.23 us -> none
where the time goes in v2:
time: 68.4 us; the launch traced here: 68.3 us
  Pallas kernels  67.6 us (99%)
    pallas_call x1, Pallas kernels, on_device_dense(): pl.pallas_call(functools.partial(step_kernel, layout, (outer, inner, part...  65.3 us
    pallas_call x1, Pallas kernels, on_device_dense(): pl.pallas_call(widen_kernel, out_shape=[jax.ShapeDtypeStruct((hidden, wid...  2.34 us

profile of v2, /device:TPU:0, one launch (start us, length us, event | category | flops | bytes accessed | tf_op | source)
XLA Modules:
  0.0 68.3 jit_solution(5716887185428159693)
XLA Ops:
  0.6 65.3 %shard_map.103 = (f32[4,32]{1,0:T(4,128)}, f32[1,1]{1,0:T(1,128)}, bf16[8,96,128]{2,1,0:T(8,128)(2,1)}) custom-call(s32[32]{0:T(128)} %length_ref.1, s32[4]{0:T(128)} %query_length_ref.1, bf16[4,32,768]{2,1,0:T(8,128)(2,1)} %query_ref.1, bf16[768,128]{1,0:T(8,128)(2,1)} %head_ref.1, f32[4,32]{1,0:T(4,128)} %teacher_ref.1, s32[4,32]{1,0:T(4,128)} %owner_ref.1, ...), custom_call_target="tpu_custom_call" | custom-call | tf_op jit(solution)/shard_map/pallas_call | solution.py:885
  65.9 2.3 %shard_map.104 = (f32[768,128]{1,0:T(8,128)}, f32[4,32]{1,0:T(4,128)}, f32[1,1]{1,0:T(1,128)}) custom-call(bf16[8,96,128]{2,1,0:T(8,128)(2,1)} %get-tuple-element.9.narrow_ref, f32[4,32]{1,0:T(4,128)} %get-tuple-element.10.picked_ref, f32[1,1]{1,0:T(1,128)} %get-tuple-element.11.sum_ref), custom_call_target="tpu_custom_call" | custom-call | tf_op jit(solution)/shard_map/pallas_call | solution.py:936

commit v3 on v2

--- a/solution.py
+++ b/solution.py
@@ -548,7 +548,8 @@
             axis=0,
         )
         until = jnp.concatenate(
-            [jnp.full((tokens, 1), length_ref[place], jnp.int32) for place in places], axis=0
+            [jnp.full((tokens, length), length_ref[place], jnp.int32) for place in places],
+            axis=0,
         )
         alive = jnp.concatenate(
             [
@@ -659,9 +660,12 @@
         return column_ref[pl.ds(pair_row(pair, queries), 1), :]
 
     def scale(group, carry):
+        found = []
         for index in range(queries):
             pair = group * queries + index
-            sent_ref[pair] = (query_part_ref[pair] * weight_of(pair)).astype(BF16)
+            found.append((query_part_ref[pair] * weight_of(pair)).astype(BF16))
+        for index in range(queries):
+            sent_ref[group * queries + index] = found[index]
         return carry
 
     def scale_far(group, carry):
@@ -690,18 +694,17 @@
         first = rank // stage.held * stage.held * queries
 
         def add(group, carry):
-            for inner_index in range(queries):
-                index = group * queries + inner_index
-                value = sent_ref[first + index].astype(F32)
-                for slot in range(stage.radix - 1):
-                    value = value + landing[slot, index].astype(F32)
-                if number:
-                    sent_ref[first + index] = value.astype(BF16)
-                else:
-                    query_part_ref[index] = value
+            names = pl.ds(group * queries, queries)
+            value = sent_ref[pl.ds(first + group * queries, queries)].astype(F32)
+            for slot in range(stage.radix - 1):
+                value = value + landing[slot, names].astype(F32)
+            if number:
+                sent_ref[pl.ds(first + group * queries, queries)] = value.astype(BF16)
+            else:
+                query_part_ref[names] = value
             return carry
 
-        lax.fori_loop(0, stage.held, add, 0)
+        lax.fori_loop(0, stage.held, add, 0, unroll=min(stage.held, 4))
 
     def placed_rows(name):
         held = emb_ref[name].astype(F32)
@@ -741,10 +744,12 @@
             pre_ref[pl.ds(index, length, stride=passages), :] = value
         return carry
 
+    joined = 2 if parts % 2 == 0 else 1
+
     def head_term(index, carry):
         head_sum_ref[...] += lax.dot_general(
-            pre_ref[pl.ds(pl.multiple_of(index * span, 8), span), :].astype(BF16),
-            held_ref[pl.ds(index * step, step)].reshape(span, hidden),
+            pre_ref[pl.ds(pl.multiple_of(index * joined * span, 8), joined * span), :].astype(BF16),
+            held_ref[pl.ds(index * joined * step, joined * step)].reshape(joined * span, hidden),
             (((0,), (0,)), ((), ())),
             preferred_element_type=F32,
         )
@@ -763,19 +768,22 @@
             lax.fori_loop(pairs // 8, pairs // 4, passage_side, total, unroll=4)
             lax.fori_loop(0, passages // 4, passage_grad, 0, unroll=2)
         if number == 0:
-            lax.fori_loop(0, parts, head_term, 0)
+            lax.fori_loop(0, parts // joined, head_term, 0)
         reduce_end(number, flight)
 
-    for index in range(queries):
-        along = query_part_ref[index]
-        pre = query_pre_ref[index]
-        inverse = normal(pre)
-        unit = pre * inverse
-        radial = jnp.sum(along * unit, axis=-1, keepdims=True)
-        grad = ((along - unit * radial) * inverse).astype(BF16)
-        head_sum_ref[...] += lax.dot_general(
-            grad, query_ref[index], (((0,), (0,)), ((), ())), preferred_element_type=F32
-        )
+    flat = (queries * tokens, width)
+    along = query_part_ref[0:queries].reshape(flat)
+    pre = query_pre_ref[...].reshape(flat)
+    inverse = normal(pre)
+    unit = pre * inverse
+    radial = jnp.sum(along * unit, axis=-1, keepdims=True)
+    grad = ((along - unit * radial) * inverse).astype(BF16)
+    head_sum_ref[...] += lax.dot_general(
+        grad,
+        query_ref[...].reshape(queries * tokens, hidden),
+        (((0,), (0,)), ((), ())),
+        preferred_element_type=F32,
+    )
 
     chunks, rows_each, _ = head_part_ref.shape
     upright = jnp.transpose(head_sum_ref[...])

time: 68.4 us -> 68.1 us (level)
  no operation moved by 1% of the time
where the time goes in v3:
time: 68.1 us; the launch traced here: 67.9 us
  Pallas kernels  67.3 us (99%)
    pallas_call x1, Pallas kernels, on_device_dense(): pl.pallas_call(functools.partial(step_kernel, layout, (outer, inner, part...  64.9 us
    pallas_call x1, Pallas kernels, on_device_dense(): pl.pallas_call(widen_kernel, out_shape=[jax.ShapeDtypeStruct((hidden, wid...  2.34 us

profile of v3, /device:TPU:0, one launch (start us, length us, event | category | flops | bytes accessed | tf_op | source)
XLA Modules:
  0.0 67.9 jit_solution(11877080600238068422)
XLA Ops:
  0.6 64.9 %shard_map.103 = (f32[4,32]{1,0:T(4,128)}, f32[1,1]{1,0:T(1,128)}, bf16[8,96,128]{2,1,0:T(8,128)(2,1)}) custom-call(s32[32]{0:T(128)} %length_ref.1, s32[4]{0:T(128)} %query_length_ref.1, bf16[4,32,768]{2,1,0:T(8,128)(2,1)} %query_ref.1, bf16[768,128]{1,0:T(8,128)(2,1)} %head_ref.1, f32[4,32]{1,0:T(4,128)} %teacher_ref.1, s32[4,32]{1,0:T(4,128)} %owner_ref.1, ...), custom_call_target="tpu_custom_call" | custom-call | tf_op jit(solution)/shard_map/pallas_call | solution.py:893
  65.6 2.3 %shard_map.104 = (f32[768,128]{1,0:T(8,128)}, f32[4,32]{1,0:T(4,128)}, f32[1,1]{1,0:T(1,128)}) custom-call(bf16[8,96,128]{2,1,0:T(8,128)(2,1)} %get-tuple-element.9.narrow_ref, f32[4,32]{1,0:T(4,128)} %get-tuple-element.10.picked_ref, f32[1,1]{1,0:T(1,128)} %get-tuple-element.11.sum_ref), custom_call_target="tpu_custom_call" | custom-call | tf_op jit(solution)/shard_map/pallas_call | solution.py:944

commit v4 on v3

--- a/solution.py
+++ b/solution.py
@@ -467,8 +467,21 @@
             loads[index].wait()
             project(index, 0)
 
+    early = stages[0]
+    relay_base = base
+    base += early.radix * (stages[1].radix - 1)
+
+    def relay(digit, turn):
+        block = emb_ref.at[pl.ds((rank + digit - early.digit) * queries, queries)]
+        sems = relay_base + turn * (stages[1].radix - 1)
+        return [
+            send(block, block, send_sems.at[sems + slot], recv_sems.at[sems + slot], device)
+            for slot, _, device in stages[1].peers()
+        ]
+
     done = 0
     flight = gather_emb(0)
+    relayed = relay(early.digit, 0)
     for number, stage in enumerate(short_stages):
         meta_flight = gather_step(stage, rank, meta_ref, 1, send_sems, recv_sems, base)
         base += stage.radix - 1
@@ -477,8 +490,14 @@
         done = until
         finish(meta_flight)
     for number in range(1, count - 1):
-        finish(flight)
-        flight = gather_emb(number)
+        if number == 1:
+            for turn, copy in enumerate(flight):
+                copy.wait()
+                relayed += relay((early.digit + early.radix - turn - 1) % early.radix, turn + 1)
+            flight = relayed
+        else:
+            finish(flight)
+            flight = gather_emb(number)
         until = parts * (number + 1) // (count - 1) if number < count - 2 else parts
         project_until(done, until)
         done = until

time: 68.1 us -> 68.1 us (level)
  no operation moved by 1% of the time
where the time goes in v4:
time: 68.1 us; the launch traced here: 67.9 us
  Pallas kernels  67.3 us (99%)
    pallas_call x1, Pallas kernels, on_device_dense(): pl.pallas_call(functools.partial(step_kernel, layout, (outer, inner, part...  65 us
    pallas_call x1, Pallas kernels, on_device_dense(): pl.pallas_call(widen_kernel, out_shape=[jax.ShapeDtypeStruct((hidden, wid...  2.34 us

profile of v4, /device:TPU:0, one launch (start us, length us, event | category | flops | bytes accessed | tf_op | source)
XLA Modules:
  0.0 67.9 jit_solution(13076974796727758350)
XLA Ops:
  0.6 65.0 %shard_map.103 = (f32[4,32]{1,0:T(4,128)}, f32[1,1]{1,0:T(1,128)}, bf16[8,96,128]{2,1,0:T(8,128)(2,1)}) custom-call(s32[32]{0:T(128)} %length_ref.1, s32[4]{0:T(128)} %query_length_ref.1, bf16[4,32,768]{2,1,0:T(8,128)(2,1)} %query_ref.1, bf16[768,128]{1,0:T(8,128)(2,1)} %head_ref.1, f32[4,32]{1,0:T(4,128)} %teacher_ref.1, s32[4,32]{1,0:T(4,128)} %owner_ref.1, ...), custom_call_target="tpu_custom_call" | custom-call | tf_op jit(solution)/shard_map/pallas_call | solution.py:912
  65.6 2.3 %shard_map.104 = (f32[768,128]{1,0:T(8,128)}, f32[4,32]{1,0:T(4,128)}, f32[1,1]{1,0:T(1,128)}) custom-call(bf16[8,96,128]{2,1,0:T(8,128)(2,1)} %get-tuple-element.9.narrow_ref, f32[4,32]{1,0:T(4,128)} %get-tuple-element.10.picked_ref, f32[1,1]{1,0:T(1,128)} %get-tuple-element.11.sum_ref), custom_call_target="tpu_custom_call" | custom-call | tf_op jit(solution)/shard_map/pallas_call | solution.py:963
